TPU v7x, 32 devices: a whole 2x2x4 slice. The times are simulated.
32 devices in a mesh: wide: 8 (over y, x, core), narrow: 4 (over z).
Axes of the slice: x: 2, y: 2, z: 4, core: 2. Of those that a mesh axis runs over, the one named last changes fastest.
Arguments:
- tokens: bfloat16 [32768, 512], P(('wide', 'narrow')), may hold values from -6 to 6
- segment_ids: int32 [32768], P(('wide', 'narrow')), may hold values from 0 to 20, as said below
- expert_picks: int32 [32768, 2], P(('wide', 'narrow')), may hold values from 0 to 7, all different within a row; in each aligned block of 1024 rows (0 to 1023, 1024 to 2047, ...) at most 271 rows name the same one
- priority_ranks: int32 [32, 1024], P(('wide', 'narrow')), may hold values from 0 to 1023, each once within a row
- gain_attn: float32 [512], replicated, may hold values from 0.1 to 1.9
- w_qkv: bfloat16 [512, 1536], replicated, may hold values from -0.25 to 0.25
- w_proj: bfloat16 [512, 512], replicated, may hold values from -2 to 2
- gain_moe: float32 [512], replicated, may hold values from 0.1 to 1.9
- w_router: bfloat16 [512, 8], replicated, may hold values from -0.25 to 0.25
- w_in: bfloat16 [8, 512, 2048], P('wide', None, 'narrow'), may hold values from -0.25 to 0.25
- w_out: bfloat16 [8, 2048, 512], P('wide', 'narrow'), may hold values from -0.75 to 0.75
- cotangent: bfloat16 [32768, 512], P(('wide', 'narrow')), may hold values from -6 to 6
Outputs:
- mixed: bfloat16 [32768, 512], P(('wide', 'narrow'))
- grad_tokens: float32 [32768, 512], P(('wide', 'narrow'))
- grad_gain_attn: float32 [512], replicated
- grad_qkv: float32 [512, 1536], replicated
- grad_proj: float32 [512, 512], replicated
- grad_gain_moe: float32 [512], replicated
- grad_router: float32 [512, 8], replicated
- grad_in: float32 [8, 512, 2048], P('wide', None, 'narrow')
- grad_out: float32 [8, 2048, 512], P('wide', 'narrow')
- kept_counts: int32 [8], replicated
- dropped_counts: int32 [8], replicated
Inputs may be any that keep to these rules, and one draw needn't show every extreme that they name: `expert_picks`: within each aligned block of 1024 tokens (one routing group) no expert is picked more than 269 + 2 times, and in some block one is picked exactly that often; a token's 2 picks differ; every expert is picked somewhere. `priority_ranks`: each row is a permutation of one routing group's positions; rank 0 comes first. `segment_ids`: each run of 1024 slots is one sequence of whole images of 49 or 144 patches, numbered from 0 up in order; the slots after the last whole image form one more segment. Some sequence holds only images of 49 patches.
All inputs are finite; a program needn't handle non-finite values.
Results may differ from a plain program's by a relative error of at most 0.015.
The roundings to bfloat16 on the way count: a program that leaves them out, or rounds other values in their place, can miss the bound.
Values may be sent and summed in bfloat16 or wider, within the bound.
A program may use at most 256 MiB of HBM per device.

v0:
```python
import jax
import jax.numpy as jnp
from jax import lax
from jax.sharding import PartitionSpec as P

D = 512
HEADS = 8
HEAD = 64
TOP = 2
SEQ = 1024
SEQS_DEV = 1
TOK_DEV = 1024


highest = lax.Precision.HIGHEST


def norm_parts(values_in):
    centered = values_in - jnp.mean(values_in, axis=-1, keepdims=True)
    variance = jnp.mean(centered * centered, axis=-1, keepdims=True)
    inverse = lax.rsqrt(variance + 1e-06)
    return (centered * inverse, inverse)


def norm_back(grad_normed, gain, normalized, inverse):
    grad_gain = jnp.sum(grad_normed * normalized, axis=0)
    scaled = grad_normed * gain
    inner = scaled - jnp.mean(scaled, axis=-1, keepdims=True)
    inner = inner - normalized * jnp.mean(scaled * normalized, axis=-1, keepdims=True)
    return (inner * inverse, grad_gain)


def exact_gelu(values_in):
    return jax.nn.gelu(values_in, approximate=False)


def route_group(picked, ranking, experts):
    group_size = picked.shape[0]
    by_rank = jnp.zeros_like(ranking).at[ranking].set(jnp.arange(group_size, dtype=jnp.int32))
    ordered = picked[by_rank].T.reshape(-1)
    onehot = (ordered[:, None] == jnp.arange(experts, dtype=jnp.int32)[None, :]).astype(jnp.int32)
    before = jnp.cumsum(onehot, axis=0) - onehot
    position = jnp.sum(before * onehot, axis=1)
    lookup = jnp.arange(picked.shape[1], dtype=jnp.int32)[None, :] * group_size + ranking[:, None]
    return position[lookup]


def scores_of(queries, key_heads, segments):
    scores = jnp.einsum(
        "sqhd,skhd->shqk", queries, key_heads, preferred_element_type=jnp.float32
    ) * HEAD ** (-0.5)
    allowed = segments[:, None, :, None] == segments[:, None, None, :]
    return jnp.where(allowed, scores, -1e30)


def expert_front(routed_rows, weight_in):
    return jnp.einsum("secd,edf->secf", routed_rows, weight_in, preferred_element_type=jnp.float32)


def expert_back(grad_rows_in, preact, weight_out):
    grad_act = jnp.einsum(
        "secd,efd->secf", grad_rows_in, weight_out, preferred_element_type=jnp.float32
    )
    unused, gelu_back = jax.vjp(exact_gelu, preact)
    return gelu_back(grad_act)[0].astype(jnp.bfloat16)


def place_rows(values_in, target, slots_total):
    feature = values_in.shape[-1]
    buffer = jnp.zeros((slots_total + 1, feature), values_in.dtype)
    return buffer.at[target.reshape(-1)].set(values_in.reshape(-1, feature))[:-1]


def fetch_rows(buffer, target):
    padded = jnp.concatenate([buffer, jnp.zeros((1, buffer.shape[-1]), buffer.dtype)], axis=0)
    return padded[target]


def per_device(
    tokens,
    segment_ids,
    expert_picks,
    priority_ranks,
    gain_attn,
    w_qkv,
    w_proj,
    gain_moe,
    w_router,
    w_in,
    w_out,
    cotangent,
):
    wide_count = lax.axis_size("wide")
    experts = w_router.shape[1]
    local_experts = experts // wide_count
    capacity = (21 * TOP * TOK_DEV + 20 * experts - 1) // (20 * experts)
    all_heads = HEADS * HEAD
    head_shape = (SEQS_DEV, SEQ, HEADS, HEAD)
    score_scale = HEAD ** (-0.5)
    segments = segment_ids.reshape(SEQS_DEV, SEQ)
    inputs = tokens.astype(jnp.float32)
    normal_attn, inverse_attn = norm_parts(inputs)
    normed_attn = (normal_attn * gain_attn).astype(jnp.bfloat16)
    packed = jnp.dot(normed_attn, w_qkv, preferred_element_type=jnp.float32).astype(jnp.bfloat16)
    queries = packed[:, :all_heads].reshape(head_shape)
    key_heads = packed[:, all_heads : 2 * all_heads].reshape(head_shape)
    value_heads = packed[:, 2 * all_heads :].reshape(head_shape)
    scores = scores_of(queries, key_heads, segments)
    score_peak = jnp.max(scores, axis=-1, keepdims=True)
    exponent = jnp.exp(scores - score_peak)
    totals = jnp.sum(exponent, axis=-1, keepdims=True)
    logsum = score_peak + jnp.log(totals)
    probs_low = (exponent / totals).astype(jnp.bfloat16)
    context = jnp.einsum(
        "shqk,skhd->sqhd", probs_low, value_heads, preferred_element_type=jnp.float32
    )
    context = context.reshape(TOK_DEV, all_heads).astype(jnp.bfloat16)
    residual = inputs + jnp.dot(context, w_proj, preferred_element_type=jnp.float32)
    normal_moe, inverse_moe = norm_parts(residual)
    normed_moe = (normal_moe * gain_moe).astype(jnp.bfloat16)
    gate_probs = jax.nn.softmax(
        jnp.dot(normed_moe, w_router, preferred_element_type=jnp.float32), axis=-1
    )
    slot_index = route_group(expert_picks, priority_ranks[0], experts)
    kept_mask = slot_index < capacity
    kept_float = kept_mask.astype(jnp.float32)
    target = jnp.where(kept_mask, expert_picks * capacity + slot_index, experts * capacity)
    picked_hot = (
        expert_picks[:, :, None] == jnp.arange(experts, dtype=jnp.int32)[None, None, :]
    ).astype(jnp.float32)
    gate_pick = jnp.sum(picked_hot * gate_probs[:, None, :], axis=-1) * kept_float
    copies = jnp.broadcast_to(normed_moe[:, None, :], (TOK_DEV, TOP, D))
    send_buffer = place_rows(copies, target, experts * capacity).reshape(
        wide_count, local_experts, capacity, D
    )
    received = lax.all_to_all(send_buffer, "wide", split_axis=0, concat_axis=0, tiled=True)
    weight_in, weight_out = (
        lax.all_gather(w_in, "narrow", axis=2, tiled=True),
        lax.all_gather(w_out, "narrow", axis=1, tiled=True),
    )
    preact = expert_front(received, weight_in)
    act_low = exact_gelu(preact).astype(jnp.bfloat16)
    outputs = jnp.einsum("secf,efd->secd", act_low, weight_out, preferred_element_type=jnp.float32)
    returned = lax.all_to_all(
        outputs.astype(jnp.bfloat16), "wide", split_axis=0, concat_axis=0, tiled=True
    )
    expert_out = fetch_rows(returned.reshape(experts * capacity, D), target).astype(jnp.float32)
    mixed = (residual + jnp.sum(gate_pick[:, :, None] * expert_out, axis=1)).astype(jnp.bfloat16)
    grad_z = cotangent.astype(jnp.float32)
    grad_gate = jnp.sum(expert_out * grad_z[:, None, :], axis=-1) * kept_float
    grad_copies = (gate_pick[:, :, None] * grad_z[:, None, :]).astype(jnp.bfloat16)
    grad_send = place_rows(grad_copies, target, experts * capacity).reshape(
        wide_count, local_experts, capacity, D
    )
    grad_received = lax.all_to_all(grad_send, "wide", split_axis=0, concat_axis=0, tiled=True)
    grad_rows_in = grad_received
    rows_again, weight_again, grad_rows_in = lax.optimization_barrier(
        (received, weight_in, grad_rows_in)
    )
    preact = expert_front(rows_again, weight_again)
    grad_preact = expert_back(grad_rows_in, preact, weight_out)
    grad_out_part = jnp.einsum(
        "secf,secd->efd", act_low, grad_rows_in, preferred_element_type=jnp.float32
    )
    grad_in_part = jnp.einsum(
        "secd,secf->edf", received, grad_preact, preferred_element_type=jnp.float32
    )
    grad_rows_out = jnp.einsum(
        "secf,edf->secd", grad_preact, weight_in, preferred_element_type=jnp.float32
    )
    grad_w_in, grad_w_out = (
        lax.psum_scatter(
            grad_in_part.astype(jnp.bfloat16), "narrow", scatter_dimension=2, tiled=True
        ).astype(jnp.float32),
        lax.psum_scatter(
            grad_out_part.astype(jnp.bfloat16), "narrow", scatter_dimension=1, tiled=True
        ).astype(jnp.float32),
    )
    grad_back = lax.all_to_all(
        grad_rows_out.astype(jnp.bfloat16), "wide", split_axis=0, concat_axis=0, tiled=True
    )
    grad_copy = fetch_rows(grad_back.reshape(experts * capacity, D), target).astype(jnp.float32)
    grad_gates = jnp.sum(picked_hot * grad_gate[:, :, None], axis=1)
    grad_logits = gate_probs * (
        grad_gates - jnp.sum(gate_probs * grad_gates, axis=-1, keepdims=True)
    )
    normed_float = normed_moe.astype(jnp.float32)
    grad_router = jnp.einsum("td,te->de", normed_float, grad_logits, precision=highest)
    grad_normed = jnp.einsum(
        "te,de->td", grad_logits, w_router.astype(jnp.float32), precision=highest
    )
    grad_normed = grad_normed + jnp.sum(grad_copy, axis=1)
    grad_residual_norm, grad_gain_moe = norm_back(grad_normed, gain_moe, normal_moe, inverse_moe)
    grad_residual = grad_z + grad_residual_norm
    grad_attn = grad_residual.astype(jnp.bfloat16)
    grad_proj = jnp.einsum("td,te->de", context, grad_attn, preferred_element_type=jnp.float32)
    grad_context = jnp.einsum("te,de->td", grad_attn, w_proj, preferred_element_type=jnp.float32)
    grad_context = grad_context.astype(jnp.bfloat16).reshape(head_shape)
    probs_again = jnp.exp(scores_of(queries, key_heads, segments) - logsum)
    probs_again_low = probs_again.astype(jnp.bfloat16)
    grad_probs = jnp.einsum(
        "sqhd,skhd->shqk", grad_context, value_heads, preferred_element_type=jnp.float32
    )
    grad_values = jnp.einsum(
        "shqk,sqhd->skhd", probs_again_low, grad_context, preferred_element_type=jnp.float32
    ).astype(jnp.bfloat16)
    grad_scores = probs_again * (
        grad_probs - jnp.sum(probs_again * grad_probs, axis=-1, keepdims=True)
    )
    grad_scores = grad_scores.astype(jnp.bfloat16)
    grad_queries = (
        jnp.einsum("shqk,skhd->sqhd", grad_scores, key_heads, preferred_element_type=jnp.float32)
        * score_scale
    ).astype(jnp.bfloat16)
    grad_keys = (
        jnp.einsum("shqk,sqhd->skhd", grad_scores, queries, preferred_element_type=jnp.float32)
        * score_scale
    ).astype(jnp.bfloat16)
    grad_packed = jnp.concatenate(
        [
            grad_queries.reshape(TOK_DEV, all_heads),
            grad_keys.reshape(TOK_DEV, all_heads),
            grad_values.reshape(TOK_DEV, all_heads),
        ],
        axis=1,
    )
    grad_qkv = jnp.einsum("td,te->de", normed_attn, grad_packed, preferred_element_type=jnp.float32)
    grad_normed_attn = jnp.einsum(
        "te,de->td", grad_packed, w_qkv, preferred_element_type=jnp.float32
    )
    grad_input_norm, grad_gain_attn = norm_back(
        grad_normed_attn, gain_attn, normal_attn, inverse_attn
    )
    grad_tokens = grad_residual + grad_input_norm
    kept_local = jnp.sum(picked_hot * kept_float[:, :, None], axis=(0, 1))
    total_local = jnp.sum(picked_hot, axis=(0, 1))
    summed = lax.psum(
        (grad_gain_attn, grad_qkv, grad_proj, grad_gain_moe, grad_router, kept_local, total_local),
        ("wide", "narrow"),
    )
    kept_counts = summed[5].astype(jnp.int32)
    dropped_counts = (summed[6] - summed[5]).astype(jnp.int32)
    return (
        mixed,
        grad_tokens,
        summed[0],
        summed[1],
        summed[2],
        summed[3],
        summed[4],
        grad_w_in,
        grad_w_out,
        kept_counts,
        dropped_counts,
    )


def solution(mesh):
    placed = (
        P(("wide", "narrow"), None),
        P(("wide", "narrow")),
        P(("wide", "narrow"), None),
        P(("wide", "narrow"), None),
        P(),
        P(),
        P(),
        P(),
        P(),
        P("wide", None, "narrow"),
        P("wide", "narrow", None),
        P(("wide", "narrow"), None),
    )
    return jax.shard_map(
        per_device,
        mesh=mesh,
        in_specs=placed,
        out_specs=(
            P(("wide", "narrow"), None),
            P(("wide", "narrow"), None),
            P(),
            P(),
            P(),
            P(),
            P(),
            P("wide", None, "narrow"),
            P("wide", "narrow", None),
            P(),
            P(),
        ),
        check_vma=False,
    )
```

profile of v0, /device:TPU:0, one launch (start us, length us, event | category | flops | bytes accessed | tf_op | source)
XLA Modules:
  0.0 713.9 jit_solution(15204804513961109076)
XLA Ops:
  20.4 11.8 %gather_fusion.1 = s32[2048]{0:T(1024)S(1)} fusion(s32[2048]{0:T(1024)S(1)} %fusion.111, s32[2048]{0:T(1024)S(1)} %broadcast_clamp_fusion.1), kind=kCustom, calls=%fused_computation.1 | custom fusion | bytes 24576 | tf_op jit(solution)/shard_map/gather | solution.py:45
  52.5 5.0 mul.289
  57.5 6.1 mul.298
  63.5 15.2 %fusion.183 = (f32[8,1024]{1,0:T(8,128)S(1)}, f32[8,1024,1024]{1,2,0:T(8,128)}) fusion(bf16[1024,8,64]{0,2,1:T(8,128)(2,1)} %bitcast.311, bf16[1024,8,64]{0,2,1:T(8,128)(2,1)} %bitcast.309, pred[1024,1024]{0,1:T(8,128)(4,1)} %broadcast_compare_fusion), kind=kOutput, calls=%fused_computation.248 | convolution fusion | flops 1098899456 | bytes 36732928 | tf_op jit(solution)/shard_map/sqhd,skhd->shqk/dot_general | solution.py:49
  78.7 13.3 %fusion = f32[8,1024]{1,0:T(8,128)S(1)} fusion(f32[8,1024,1024]{1,2,0:T(8,128)} %get-tuple-element.100, f32[8,1024]{1,0:T(8,128)S(1)} %get-tuple-element.99), kind=kLoop, calls=%fused_computation.13 | loop fusion | flops 16769024 | bytes 33619968 | tf_op jit(solution)/shard_map/reduce_sum | solution.py:111
  92.1 13.7 %fusion.98 = bf16[8,64,1024]{2,1,0:T(8,128)(2,1)S(1)} fusion(bf16[1024,8,64]{0,2,1:T(8,128)(2,1)S(1)} %bitcast.317, f32[8,1024,1024]{1,2,0:T(8,128)} %get-tuple-element.100, f32[8,1024]{1,0:T(8,128)S(1)} %fusion, f32[8,1024]{1,0:T(8,128)S(1)} %get-tuple-element.99), kind=kOutput, calls=%fused_computation.130 | convolution fusion | flops 1099431936 | bytes 35717120 | tf_op jit(solution)/shard_map/shqk,skhd->sqhd/dot_general | solution.py:114
  109.8 12.5 %scatter_custom_fusion.2 = bf16[2153,512]{1,0:T(8,128)(2,1)} fusion(s32[2048]{0:T(1024)S(1)} %bitcast.332, f32[2048,512]{1,0:T(8,128)} %mul.298, f32[2048]{0:T(1024)S(1)} %mul.296, bf16[]{:T(256)} %constant.16.clone.1), kind=kCustom, calls=%fused_computation.107 | custom fusion | flops 2097152 | bytes 6407170 | tf_op jit(solution)/shard_map/scatter | solution.py:71
  129.1 5.2 all-to-all-start.2
  144.3 11.6 %scatter_custom_fusion.1 = bf16[2153,512]{1,0:T(8,128)(2,1)} fusion(s32[2048]{0:T(1024)S(1)} %bitcast.333, bf16[2048,512]{1,0:T(8,128)(2,1)} %reshape.502, bf16[]{:T(256)} %constant.16.clone.1), kind=kCustom, calls=%fused_computation.134 | custom fusion | bytes 2205184 | tf_op jit(solution)/shard_map/scatter | solution.py:71
  170.2 25.0 %all-to-all-done = bf16[8,1,269,512]{3,2,1,0:T(8,128)(2,1)} async-done(((bf16[8,1,269,512]{3,2,1,0:T(8,128)(2,1)}), bf16[8,1,269,512]{3,2,1,0:T(8,128)(2,1)}, u32[]{:S(2)}, u32[]{:S(2)}) %all-to-all-start) | async-done | bytes 2203680 | tf_op jit(solution)/shard_map/all_to_all | solution.py:136
  195.2 7.1 fusion.71
  202.3 6.1 copy-done.49
  208.4 43.0 %fusion.55 = bf16[1,2048,512]{2,1,0:T(8,128)(2,1)} fusion(f32[8,269,2048]{2,1,0:T(8,128)S(1)} %fusion.71, bf16[8,1,269,512]{3,2,1,0:T(8,128)(2,1)} %all-to-all-done.2), kind=kOutput, calls=%fused_computation.84 | convolution fusion | flops 4800593920 | bytes 21929984 | tf_op jit(solution)/shard_map/secf,secd->efd/dot_general | solution.py:162
  251.4 42.5 %convert_bitcast_fusion.1 = bf16[8,1,269,512]{3,2,1,0:T(8,128)(2,1)} fusion(bf16[1,2048,512]{2,1,0:T(8,128)(2,1)} %all-gather.5.cloned.1.call-done, f32[8,269,2048]{2,1,0:T(8,128)} %copy-done.49), kind=kOutput, calls=%fused_computation.99 | convolution fusion | flops 4800647168 | bytes 21929984 | tf_op jit(solution)/shard_map/secf,efd->secd/dot_general | solution.py:143
  298.5 7.3 %fusion.68 = f32[2048,8,269]{0,2,1:T(8,128)S(1)} fusion(bf16[8,1,269,512]{3,2,1,0:T(8,128)(2,1)} %all-to-all-done, bf16[1,512,2048]{2,1,0:T(8,128)(2,1)} %all-gather.3.cloned.1.call-done), kind=kOutput, calls=%fused_computation.93 | convolution fusion | flops 4513071104 | bytes 21929984 | tf_op jit(solution)/shard_map/secd,edf->secf/dot_general | solution.py:57
  305.8 46.5 %fusion.9 = bf16[8,1,269,2048]{3,2,0,1:T(8,128)(2,1)} fusion(f32[2048,8,269]{0,2,1:T(8,128)S(1)} %fusion.68, bf16[8,1,269,512]{3,2,1,0:T(8,128)(2,1)} %all-to-all-done.2, bf16[1,2048,512]{2,1,0:T(8,128)(2,1)S(1)} %copy-done.48), kind=kOutput, calls=%fused_computation.24 | convolution fusion | flops 4830396416 | bytes 30744576 | tf_op jit(solution)/shard_map/secd,efd->secf/dot_general | solution.py:61
  352.3 10.0 %convert_bitcast_fusion = bf16[8,1,269,512]{3,2,1,0:T(8,128)(2,1)} fusion(bf16[1,512,2048]{2,1,0:T(8,128)(2,1)S(1)} %copy-done.47, bf16[8,1,269,2048]{3,2,0,1:T(8,128)(2,1)} %fusion.9), kind=kOutput, calls=%fused_computation.98 | convolution fusion | flops 4514172928 | bytes 13115392 | tf_op jit(solution)/shard_map/secf,edf->secd/dot_general | solution.py:168
  366.8 9.3 %fusion.52 = bf16[1,512,2048]{2,1,0:T(8,128)(2,1)} fusion(bf16[8,1,269,2048]{3,2,0,1:T(8,128)(2,1)} %fusion.9, bf16[8,1,269,512]{3,2,1,0:T(8,128)(2,1)} %all-to-all-done), kind=kOutput, calls=%fused_computation.83 | convolution fusion | flops 4514119680 | bytes 13115392 | tf_op jit(solution)/shard_map/secd,secf->edf/dot_general | solution.py:165
  383.1 11.4 %gather_fusion.2 = bf16[2048,512]{1,0:T(8,128)(2,1)} fusion(bf16[2153,512]{1,0:T(8,128)(2,1)} %concatenate.9, s32[2048]{0:T(1024)S(1)} %copy-done.1), kind=kCustom, calls=%fused_computation.2 | custom fusion | bytes 4202496 | tf_op jit(solution)/shard_map/gather | solution.py:76
  394.5 5.5 reshape.520
  400.0 11.2 %multiply_reduce_fusion.1 = (f32[1024,2]{1,0:T(8,128)S(1)}, f32[1024,512]{1,0:T(8,128)}) fusion(f32[1024,2,512]{2,1,0:T(2,128)} %reshape.520, f32[1024,512]{1,0:T(8,128)} %copy.137, f32[1024,2]{1,0:T(8,128)S(1)} %copy-done.12), kind=kLoop, calls=%fused_computation.76 | loop fusion | flops 3667968 | bytes 8404992 | tf_op jit(solution)/shard_map/reduce_sum | solution.py:150
  421.3 11.2 %gather_fusion.3 = bf16[2048,512]{1,0:T(8,128)(2,1)} fusion(bf16[2153,512]{1,0:T(8,128)(2,1)} %concatenate.10, s32[2048]{0:T(1024)S(1)} %copy-done.1), kind=kCustom, calls=%fused_computation.3 | custom fusion | bytes 4202496 | tf_op jit(solution)/shard_map/gather | solution.py:76
  432.5 5.5 reshape.521
  438.1 8.5 %reduce_sum.210 = f32[1024,512]{1,0:T(8,128)} reduce(f32[1024,2,512]{2,1,0:T(2,128)} %reshape.521, f32[]{:T(128)} %constant.43.clone.1), dimensions={1}, to_apply=%region_19.20 | reduce | flops 524288 | bytes 6291460 | tf_op jit(solution)/shard_map/reduce_sum | solution.py:192
  460.1 22.5 %multiply_reduce_fusion = (f32[8,1024]{1,0:T(8,128)S(1)}, f32[8,1024,1024]{1,2,0:T(8,128)}) fusion(f32[8,1024,1024]{1,2,0:T(8,128)} %get-tuple-element.100, f32[8,1024]{1,0:T(8,128)S(1)} %copy-done.18, bf16[1024,8,64]{0,2,1:T(8,128)(2,1)S(1)} %bitcast.313, bf16[1024,8,64]{0,2,1:T(8,128)(2,1)S(1)} %bitcast.318), kind=kOutput, calls=%fused_computation.8 | convolution fusion | flops 1098899456 | bytes 69271552 | tf_op jit(solution)/shard_map/sqhd,skhd->shqk/dot_general | solution.py:201
  482.6 28.1 %multiply_convert_fusion = bf16[8,1024,1024]{1,2,0:T(8,128)(2,1)} fusion(f32[8,1024,1024]{1,2,0:T(8,128)} %get-tuple-element.107, f32[8,1024,1024]{1,2,0:T(8,128)} %get-tuple-element.100, f32[8,1024]{1,0:T(8,128)S(1)} %get-tuple-element.106, f32[8,1024]{1,0:T(8,128)S(1)} %copy-done.18), kind=kLoop, calls=%fused_computation.7 | loop fusion | flops 33554432 | bytes 83951616 | tf_op jit(solution)/shard_map/convert_element_type | solution.py:210
  514.5 12.3 %multiply_convert_fusion.3 = bf16[8,64,1024]{2,1,0:T(8,128)(2,1)} fusion(bf16[1024,8,64]{0,2,1:T(8,128)(2,1)} %bitcast.312, bf16[8,1024,1024]{1,2,0:T(8,128)(2,1)} %multiply_convert_fusion), kind=kOutput, calls=%fused_computation.114 | convolution fusion | flops 1074790400 | bytes 18874368 | tf_op jit(solution)/shard_map/shqk,sqhd->skhd/dot_general | solution.py:216
  526.8 9.8 %multiply_convert_fusion.4 = bf16[8,64,1024]{2,1,0:T(8,128)(2,1)} fusion(bf16[1024,8,64]{0,2,1:T(8,128)(2,1)S(1)} %bitcast.310, bf16[8,1024,1024]{1,2,0:T(8,128)(2,1)} %multiply_convert_fusion), kind=kOutput, calls=%fused_computation.115 | convolution fusion | flops 1074790400 | bytes 18874368 | tf_op jit(solution)/shard_map/shqk,skhd->sqhd/dot_general | solution.py:212
  536.6 14.6 %fusion.95 = bf16[8,64,1024]{2,1,0:T(8,128)(2,1)} fusion(bf16[1024,8,64]{0,2,1:T(8,128)(2,1)} %bitcast.314, f32[8,1024,1024]{1,2,0:T(8,128)} %get-tuple-element.100, f32[8,1024]{1,0:T(8,128)S(1)} %copy-done.18), kind=kOutput, calls=%fused_computation.128 | convolution fusion | flops 1091043328 | bytes 35684352 | tf_op jit(solution)/shard_map/shqk,sqhd->skhd/dot_general | solution.py:204
  551.2 5.4 fusion.99
  570.2 42.0 %all-reduce.2 = (f32[512]{0:T(512)}, f32[512]{0:T(512)}, f32[512,8]{0,1:T(8,128)}, f32[8]{0:T(128)S(1)}, f32[8]{0:T(128)S(1)}) all-reduce(f32[512]{0:T(512)S(1)} %get-tuple-element.76, f32[512]{0:T(512)S(1)} %get-tuple-element.72, f32[512,8]{0,1:T(8,128)S(1)} %fusion.115, ...), channel_id=1, replica_groups=mesh['wide'=8,'narrow'=4] {'wide','narrow'}, use_global_device_ids=true, to_apply=%region_26.27 | all-reduce | flops 5136 | bytes 41088 | tf_op jit(solution)/shard_map/psum | solution.py:237
  617.0 84.1 %all-reduce.6.cloned.1.call-done = (f32[512,1536]{1,0:T(8,128)}, f32[512,512]{1,0:T(8,128)}) async-done(((f32[512,1536]{1,0:T(8,128)}, f32[512,512]{1,0:T(8,128)}), (f32[512,1536]{1,0:T(8,128)}, f32[512,512]{1,0:T(8,128)})) %all-reduce.6.cloned.1.call-update) | async-done | bytes 4194320 | tf_op jit(solution)/shard_map/psum | solution.py:237
  (208 shorter events, 136.0 us)
Async XLA Ops:
  7.2 34.8 %copy-start = (bf16[512,1536]{1,0:T(8,128)(2,1)S(1)}, bf16[512,1536]{1,0:T(8,128)(2,1)}, u32[]{:S(2)}) copy-start(bf16[512,1536]{1,0:T(8,128)(2,1)} %param.17) | copy-start | bytes 4718596
  32.9 135.5 %copy-start.23 = (s32[1024,2]{0,1:T(2,128)}, s32[1024,2]{0,1:T(2,128)S(1)}, u32[]{:S(2)}) copy-start(s32[1024,2]{0,1:T(2,128)S(1)} %copy.127) | copy-start | bytes 24580
  35.0 70.8 %copy-start.5 = (bf16[1024,512]{0,1:T(8,128)(2,1)}, bf16[1024,512]{0,1:T(8,128)(2,1)S(1)}, u32[]{:S(2)}) copy-start(bf16[1024,512]{0,1:T(8,128)(2,1)S(1)} %copy.119) | copy-start | bytes 3145732
  35.2 22.3 %copy-start.33 = (f32[1024]{0:T(1024)}, f32[1024]{0:T(1024)S(1)}, u32[]{:S(2)}) copy-start(f32[1024]{0:T(1024)S(1)} %broadcast_multiply_fusion.5) | copy-start | bytes 12292
  108.2 50.9 %copy-start.7 = (bf16[1024,512]{0,1:T(8,128)(2,1)}, bf16[1024,512]{0,1:T(8,128)(2,1)S(1)}, u32[]{:S(2)}) copy-start(bf16[1024,512]{0,1:T(8,128)(2,1)S(1)} %multiply_convert_fusion.5) | copy-start | bytes 3145732
  109.5 49.6 %copy-start.11 = (f32[1024,2]{1,0:T(8,128)}, f32[1024,2]{1,0:T(8,128)S(1)}, u32[]{:S(2)}) copy-start(f32[1024,2]{1,0:T(8,128)S(1)} %copy.128) | copy-start | bytes 24580
  129.1 33.6 %all-to-all-start.2 = ((bf16[8,1,269,512]{3,2,1,0:T(8,128)(2,1)}), bf16[8,1,269,512]{3,2,1,0:T(8,128)(2,1)}, u32[]{:S(2)}, u32[]{:S(2)}) async-start(bf16[8,1,269,512]{3,2,1,0:T(8,128)(2,1)} %bitcast.316), calls=%async_computation.2 | async-start | bytes 4456448 | tf_op jit(solution)/shard_map/all_to_all | solution.py:155
  134.3 60.9 %all-gather.3.cloned.1.call-start = ((), (), s32[]{:S(2)}) async-start(), calls=%async_computation.6 | async-start | bytes 2621440 | tf_op jit(solution)/shard_map/all_gather | solution.py:138
  162.7 32.5 %all-to-all-start = ((bf16[8,1,269,512]{3,2,1,0:T(8,128)(2,1)}), bf16[8,1,269,512]{3,2,1,0:T(8,128)(2,1)}, u32[]{:S(2)}, u32[]{:S(2)}) async-start(bf16[8,1,269,512]{3,2,1,0:T(8,128)(2,1)} %bitcast.315), calls=%async_computation | async-start | bytes 4456448 | tf_op jit(solution)/shard_map/all_to_all | solution.py:136
  167.1 84.3 %all-gather.5.cloned.1.call-start = ((), (), s32[]{:S(2)}) async-start(), calls=%async_computation.7 | async-start | bytes 2621440 | tf_op jit(solution)/shard_map/all_gather | solution.py:139
  167.8 444.9 %reduce-scatter.5.cloned.1.call-start = ((), (), s32[]{:S(2)}) async-start(), calls=%async_computation.9 | async-start | bytes 2621440 | tf_op jit(solution)/shard_map/reduce_scatter | solution.py:175
  293.9 68.4 %all-to-all-start.1 = ((bf16[8,1,269,512]{3,2,1,0:T(8,128)(2,1)}), bf16[8,1,269,512]{3,2,1,0:T(8,128)(2,1)}, u32[]{:S(2)}, u32[]{:S(2)}) async-start(bf16[8,1,269,512]{3,2,1,0:T(8,128)(2,1)} %convert_bitcast_fusion.1), calls=%async_computation.1 | async-start | bytes 4456448 | tf_op jit(solution)/shard_map/all_to_all | solution.py:144
  305.8 46.5 %copy-start.47 = (bf16[1,512,2048]{2,1,0:T(8,128)(2,1)S(1)}, bf16[1,512,2048]{2,1,0:T(8,128)(2,1)}, u32[]{:S(2)}) copy-start(bf16[1,512,2048]{2,1,0:T(8,128)(2,1)} %all-gather.3.cloned.1.call-done) | copy-start | bytes 6291460
  362.3 52.2 %all-to-all-start.3 = ((bf16[8,1,269,512]{3,2,1,0:T(8,128)(2,1)}), bf16[8,1,269,512]{3,2,1,0:T(8,128)(2,1)}, u32[]{:S(2)}, u32[]{:S(2)}) async-start(bf16[8,1,269,512]{3,2,1,0:T(8,128)(2,1)} %convert_bitcast_fusion), calls=%async_computation.3 | async-start | bytes 4456448 | tf_op jit(solution)/shard_map/all_to_all | solution.py:179
  366.8 248.1 %reduce-scatter.3.cloned.1.call-start = ((), (), s32[]{:S(2)}) async-start(), calls=%async_computation.8 | async-start | bytes 2621440 | tf_op jit(solution)/shard_map/reduce_scatter | solution.py:172
  376.1 23.9 %copy-start.12 = (f32[1024,2]{1,0:T(8,128)S(1)}, f32[1024,2]{1,0:T(8,128)}, u32[]{:S(2)}) copy-start(f32[1024,2]{1,0:T(8,128)} %copy-done.11) | copy-start | bytes 24580
  376.1 325.0 %all-reduce.6.cloned.1.call-start = ((), (), s32[]{:S(2)}) async-start(), calls=%async_computation.10 | async-start | bytes 8388608 | tf_op jit(solution)/shard_map/psum | solution.py:237
  383.1 31.1 %copy-start.24 = (s32[1024,2]{0,1:T(2,128)S(1)}, s32[1024,2]{0,1:T(2,128)}, u32[]{:S(2)}) copy-start(s32[1024,2]{0,1:T(2,128)} %copy-done.23) | copy-start | bytes 24580
  383.1 31.2 %copy-start.26 = (s32[1024,2]{0,1:T(2,128)S(1)}, s32[1024,2]{0,1:T(2,128)}, u32[]{:S(2)}) copy-start(s32[1024,2]{0,1:T(2,128)} %param.14) | copy-start | bytes 24580
  383.1 31.2 %copy-start.39 = (f32[1024,2]{0,1:T(2,128)S(1)}, f32[1024,2]{0,1:T(2,128)}, u32[]{:S(2)}) copy-start(f32[1024,2]{0,1:T(2,128)} %fusion.181) | copy-start | bytes 24580
  383.1 31.3 %copy-start.22 = (f32[1024,8]{0,1:T(8,128)S(1)}, f32[1024,8]{0,1:T(8,128)}, u32[]{:S(2)}) copy-start(f32[1024,8]{0,1:T(8,128)} %copy-done.21) | copy-start | bytes 98308
  383.1 31.3 %copy-start.32 = (f32[1024]{0:T(1024)S(1)}, f32[1024]{0:T(1024)}, u32[]{:S(2)}) copy-start(f32[1024]{0:T(1024)} %copy-done.31) | copy-start | bytes 12292
  383.1 31.3 %copy-start.36 = (f32[1024]{0:T(1024)S(1)}, f32[1024]{0:T(1024)}, u32[]{:S(2)}) copy-start(f32[1024]{0:T(1024)} %copy-done.35) | copy-start | bytes 12292
  421.3 28.4 %copy-start.20 = (f32[1024,8]{0,1:T(8,128)S(1)}, f32[1024,8]{0,1:T(8,128)}, u32[]{:S(2)}) copy-start(f32[1024,8]{0,1:T(8,128)} %copy-done.19) | copy-start | bytes 98308
  421.3 28.4 %copy-start.28 = (f32[1024]{0:T(1024)S(1)}, f32[1024]{0:T(1024)}, u32[]{:S(2)}) copy-start(f32[1024]{0:T(1024)} %copy-done.27) | copy-start | bytes 12292
  421.3 28.4 %copy-start.30 = (f32[1024]{0:T(1024)S(1)}, f32[1024]{0:T(1024)}, u32[]{:S(2)}) copy-start(f32[1024]{0:T(1024)} %copy-done.29) | copy-start | bytes 12292
  421.3 28.4 %copy-start.38 = (bf16[512,8]{0,1:T(8,128)(2,1)S(1)}, bf16[512,8]{0,1:T(8,128)(2,1)}, u32[]{:S(2)}) copy-start(bf16[512,8]{0,1:T(8,128)(2,1)} %param.20) | copy-start | bytes 24580
  421.3 28.4 %copy-start.41 = (f32[512]{0:T(512)S(1)}, f32[512]{0:T(512)}, u32[]{:S(2)}) copy-start(f32[512]{0:T(512)} %param.19) | copy-start | bytes 6148
  421.3 32.4 %copy-start.10 = (bf16[1024,512]{0,1:T(8,128)(2,1)S(1)}, bf16[1024,512]{0,1:T(8,128)(2,1)}, u32[]{:S(2)}) copy-start(bf16[1024,512]{0,1:T(8,128)(2,1)} %copy.136) | copy-start | bytes 3145732
  432.5 26.8 %copy-start.17 = (bf16[512,512]{1,0:T(8,128)(2,1)S(1)}, bf16[512,512]{1,0:T(8,128)(2,1)}, u32[]{:S(2)}) copy-start(bf16[512,512]{1,0:T(8,128)(2,1)} %param.18) | copy-start | bytes 1572868
  432.5 27.6 %copy-start.18 = (f32[8,1024]{1,0:T(8,128)S(1)}, f32[8,1024]{1,0:T(8,128)}, u32[]{:S(2)}) copy-start(f32[8,1024]{1,0:T(8,128)} %log_add_fusion) | copy-start | bytes 98308
  460.1 22.6 %copy-start.9 = (bf16[1024,512]{0,1:T(8,128)(2,1)}, bf16[1024,512]{0,1:T(8,128)(2,1)S(1)}, u32[]{:S(2)}) copy-start(bf16[1024,512]{0,1:T(8,128)(2,1)S(1)} %convolution_convert_fusion.1) | copy-start | bytes 3145732
  (27 other events, 267.1 us)
Sparse Core Ops, SparseCore 0:
  136.7 48.1 all-gather.2
  186.5 44.6 all-gather.4
  251.5 43.8 reduce-scatter.4
  376.3 46.0 reduce-scatter.2
  556.8 144.3 all-reduce.5
where the time goes:
time: 725 us; the launch traced here: 714 us
  matrix products  277 us (38%)
  local copies, waits for them, and re-layouts  157 us (22%)
  waiting for transfers between devices  111 us (15%)
  other arithmetic  93.9 us (13%)
  blocking collectives  42 us (6%)
  starting transfers between devices  18.8 us (3%)
  between operations  14.8 us (2%)
    psum x1, waiting for transfers between devices, per_device(): lax.psum((grad_gain_attn, grad_qkv, grad_proj, grad_gain_moe, grad_router...  84.1 us
    dot_general x1, matrix products, expert_back(): jnp.einsum('secd,efd->secf', grad_rows_in, weight_out, preferred_element_...  46.5 us
    dot_general x1, matrix products, per_device(): jnp.einsum('secf,secd->efd', act_low, grad_rows_in, preferred_element_typ...  43 us
    dot_general x1, matrix products, per_device(): jnp.einsum('secf,efd->secd', act_low, weight_out, preferred_element_type=...  42.5 us
    psum x1, blocking collectives, per_device(): lax.psum((grad_gain_attn, grad_qkv, grad_proj, grad_gain_moe, grad_router...  42 us
    convert_element_type x1, other arithmetic, per_device(): grad_scores = grad_scores.astype(jnp.bfloat16)  28.1 us
    unnamed x108, local copies, waits for them, and re-layouts  25.1 us
    all_to_all x1, waiting for transfers between devices, per_device(): lax.all_to_all(send_buffer, 'wide', split_axis=0, concat_axis=0, tiled=True)  25 us
  transfers between devices with their start and end apart: 9, of which 2 were waited for; matrix products, arithmetic and copies ran while one was open for 55% of the time, Pallas kernels for 0%

commit v1 on v0

v1 whole, which is shorter than its diff:
```python
import functools

import jax
import jax.numpy as jnp
from jax import lax
from jax.experimental import pallas as pl
from jax.experimental.pallas import tpu as pltpu
from jax.sharding import PartitionSpec as P

D = 512
HEADS = 8
HEAD = 64
PAIRS = HEADS // 2
PAIR = 2 * HEAD
TOP = 2
SEQ = 1024
TOK_DEV = 1024
LANES = 128
QB = 128
WINDOW = 432
TILE = 256
MIB = 1024 * 1024

f32 = jnp.float32
bf16 = jnp.bfloat16
NT = (((1,), (1,)), ((), ()))
TN = (((0,), (0,)), ((), ()))


def dot(a, b):
    return jnp.dot(a, b, preferred_element_type=f32)


def dot_nt(a, b):
    return lax.dot_general(a, b, NT, preferred_element_type=f32)


def dot_tn(a, b):
    return lax.dot_general(a, b, TN, preferred_element_type=f32)


def iota(shape, dim):
    return lax.broadcasted_iota(jnp.int32, shape, dim)


def norm_parts(values_in):
    centered = values_in - jnp.mean(values_in, axis=-1, keepdims=True)
    variance = jnp.mean(centered * centered, axis=-1, keepdims=True)
    inverse = lax.rsqrt(variance + 1e-06)
    return (centered * inverse, inverse)


def norm_back(grad_normed, gain, normalized, inverse):
    grad_gain = jnp.sum(grad_normed * normalized, axis=0, keepdims=True)
    scaled = grad_normed * gain
    inner = scaled - jnp.mean(scaled, axis=-1, keepdims=True)
    inner = inner - normalized * jnp.mean(scaled * normalized, axis=-1, keepdims=True)
    return (inner * inverse, grad_gain)


def split2(values_in):
    high = values_in.astype(bf16)
    low = (values_in - high.astype(f32)).astype(bf16)
    return high, low


def row_to_col(row):
    n = row.shape[1]
    return jnp.transpose(jnp.broadcast_to(row, (LANES, n)))[:, :1]


def route_kernel(experts, capacity, picks, ranks, cot, slot_col, slot_row, counts, gz_send):
    tokens = ranks.shape[1]
    padded = gz_send.shape[1]
    rank_row = ranks[...].astype(f32)
    rank_col = row_to_col(rank_row)
    lane = iota((tokens, LANES), 1)
    pick0 = picks[:, 0:1]
    pick1 = picks[:, 1:2]
    hot = jnp.where(lane == jnp.where(lane < experts, pick0, pick1 + experts), 1.0, 0.0).astype(f32)
    before = (rank_row < rank_col).astype(f32).astype(bf16)
    earlier = dot(before, hot.astype(bf16))
    total = jnp.sum(hot, axis=0, keepdims=True)
    total = jnp.broadcast_to(total, (8, LANES))
    lane8 = iota((8, LANES), 1)
    first = jnp.where(lane8 < experts, total, 0.0)
    earlier = earlier + pltpu.roll(first, experts, axis=1)[:1]
    kept = (hot > 0.5) & (earlier < float(capacity))
    slots = jnp.where(kept, earlier, -1.0)
    slots = jnp.maximum(slots, pltpu.roll(slots, LANES - experts, axis=1))
    slots = jnp.where(lane < experts, slots, -1.0)
    slot_col[...] = slots
    slot_row[...] = jnp.transpose(slots)[:experts]
    kept_lane = jnp.sum(jnp.where(slots >= 0.0, 1.0, 0.0), axis=0, keepdims=True)
    both = total + pltpu.roll(total, LANES - experts, axis=1)
    both = jnp.where(lane8 < experts, both, 0.0)
    sub8 = iota((8, LANES), 0)
    counts[...] = jnp.where(sub8 == 0, kept_lane, jnp.where(sub8 == 1, both, 0.0))

    @pl.loop(0, experts)
    def _(e):
        chosen = iota((padded, tokens), 0).astype(f32) == slot_row[pl.ds(e, 1), :]
        gz_send[e] = dot(chosen.astype(f32).astype(bf16), cot[...]).astype(bf16)


def route(picks, ranks, cot, experts, capacity, padded):
    tokens = picks.shape[0]
    return pl.pallas_call(
        functools.partial(route_kernel, experts, capacity),
        out_shape=(
            jax.ShapeDtypeStruct((tokens, LANES), f32),
            jax.ShapeDtypeStruct((experts, tokens), f32),
            jax.ShapeDtypeStruct((8, LANES), f32),
            jax.ShapeDtypeStruct((experts, padded, D), bf16),
        ),
        compiler_params=pltpu.CompilerParams(vmem_limit_bytes=40 * MIB),
        cost_estimate=pl.CostEstimate(
            flops=2 * experts * padded * tokens * D, bytes_accessed=6 * MIB, transcendentals=0
        ),
        name="route",
    )(picks, ranks, cot)


def stack_heads(block):
    lane = iota(block.shape, 1)
    zero = jnp.zeros_like(block)
    return jnp.concatenate(
        [jnp.where(lane < HEAD, block, zero), jnp.where(lane < HEAD, zero, block)], axis=0
    )


def unstack_cols(stacked):
    row = iota((PAIR, QB), 0)
    picked = jnp.where(row < HEAD, stacked[:, :QB], stacked[:, QB:])
    return jnp.transpose(picked)


def window_bias(seg_col, seg_row, low, width, query):
    same = seg_col[pl.ds(low, width), :] == seg_row[:, pl.ds(query, QB)]
    half = jnp.where(same, 0.0, -1e30).astype(f32)
    return jnp.concatenate([half, half], axis=1)


def by_window(windows, block, body):
    low = windows[block]
    fits = windows[block + SEQ // QB]

    @pl.when(fits == 1)
    def _():
        body(pl.multiple_of(low, 16), WINDOW)

    @pl.when(fits != 1)
    def _():
        body(0, SEQ)


def forward_kernel(
    experts,
    windows,
    tok,
    seg,
    gain_attn,
    w_qkv,
    w_proj,
    gain_moe,
    w_router,
    slot_row,
    normed_attn,
    packed,
    context,
    lse,
    residual,
    normed_moe,
    gates,
    rows_send,
    seg_col,
    seg_row,
    router,
    gate_row,
    gate_slot,
):
    tokens = tok.shape[0]
    padded = rows_send.shape[1]
    seg_row[...] = seg[...].astype(f32)
    seg_col[...] = jnp.transpose(jnp.broadcast_to(seg_row[...], (LANES, tokens)))
    router[...] = jnp.zeros_like(router)
    router[:, :experts] = w_router[...]

    @pl.loop(0, tokens // TILE)
    def _(i):
        rows = pl.ds(pl.multiple_of(i * TILE, TILE), TILE)
        normal, unused = norm_parts(tok[rows, :].astype(f32))
        normed = (normal * gain_attn[...]).astype(bf16)
        normed_attn[rows, :] = normed
        packed[rows, :] = dot(normed, w_qkv[...]).astype(bf16)

    @pl.loop(0, tokens // QB)
    def _(block):
        query = pl.multiple_of(block * QB, QB)

        def body(low, width):
            bias = window_bias(seg_col, seg_row, low, width, query)
            for pair in range(PAIRS):
                cols = pair * PAIR
                q = stack_heads(packed[pl.ds(query, QB), cols : cols + PAIR]) * HEAD ** (-0.5)
                k = packed[pl.ds(low, width), D + cols : D + cols + PAIR]
                v = packed[pl.ds(low, width), 2 * D + cols : 2 * D + cols + PAIR]
                scores = dot_nt(k, q.astype(bf16)) + bias
                peak = jnp.max(scores, axis=0, keepdims=True)
                exponent = jnp.exp(scores - peak)
                totals = jnp.sum(exponent, axis=0, keepdims=True)
                probs_low = (exponent * (1.0 / totals)).astype(bf16)
                lse[pl.ds(block, 1), pair, :] = peak + jnp.log(totals)
                mixed = dot_tn(v, probs_low)
                context[pl.ds(query, QB), cols : cols + PAIR] = unstack_cols(mixed).astype(bf16)

        by_window(windows, block, body)

    @pl.loop(0, tokens // TILE)
    def _(i):
        rows = pl.ds(pl.multiple_of(i * TILE, TILE), TILE)
        rest = tok[rows, :].astype(f32) + dot(context[rows, :], w_proj[...])
        residual[rows, :] = rest
        normal, unused = norm_parts(rest)
        normed = (normal * gain_moe[...]).astype(bf16)
        normed_moe[rows, :] = normed
        logits = dot(normed, router[...])
        logits = jnp.where(iota(logits.shape, 1) < experts, logits, -1e30)
        exponent = jnp.exp(logits - jnp.max(logits, axis=1, keepdims=True))
        gates[rows, :] = exponent / jnp.sum(exponent, axis=1, keepdims=True)

    gate_row[...] = jnp.transpose(gates[...])[:experts]
    gate_slot[...] = jnp.zeros_like(gate_slot)

    @pl.loop(0, experts)
    def _(e):
        chosen = iota((padded, tokens), 0).astype(f32) == slot_row[pl.ds(e, 1), :]
        chosen = chosen.astype(f32).astype(bf16)
        rows_send[e] = dot(chosen, normed_moe[...]).astype(bf16)
        gate = gate_row[pl.ds(e, 1), :]
        high, middle = split2(gate)
        low = (gate - high.astype(f32) - middle.astype(f32)).astype(bf16)
        three = jnp.concatenate(
            [high.astype(f32), middle.astype(f32), low.astype(f32), jnp.zeros((5, tokens), f32)], axis=0
        )
        gate_slot[:, :padded] = dot_nt(three.astype(bf16), chosen)
        tail = rows_send[e, padded - 16 :, :].astype(f32)
        sub = iota(tail.shape, 0)
        for part in range(3):
            tail = jnp.where(sub == 13 + part, gate_slot[part : part + 1, :], tail)
        rows_send[e, padded - 16 :, :] = tail.astype(bf16)


def forward(windows, tok, seg, gain_attn, w_qkv, w_proj, gain_moe, w_router, slot_row, padded):
    tokens = tok.shape[0]
    experts = w_router.shape[1]
    vmem = pl.BlockSpec(memory_space=pltpu.VMEM)
    return pl.pallas_call(
        functools.partial(forward_kernel, experts),
        in_specs=[pl.BlockSpec(memory_space=pltpu.SMEM)] + [vmem] * 8,
        out_shape=(
            jax.ShapeDtypeStruct((tokens, D), bf16),
            jax.ShapeDtypeStruct((tokens, 3 * D), bf16),
            jax.ShapeDtypeStruct((tokens, D), bf16),
            jax.ShapeDtypeStruct((tokens // QB, PAIRS, 2 * QB), f32),
            jax.ShapeDtypeStruct((tokens, D), f32),
            jax.ShapeDtypeStruct((tokens, D), bf16),
            jax.ShapeDtypeStruct((tokens, LANES), f32),
            jax.ShapeDtypeStruct((experts, padded, D), bf16),
        ),
        scratch_shapes=[
            pltpu.VMEM((tokens, LANES), f32),
            pltpu.VMEM((1, tokens), f32),
            pltpu.VMEM((D, LANES), bf16),
            pltpu.VMEM((experts, tokens), f32),
            pltpu.VMEM((8, D), f32),
        ],
        compiler_params=pltpu.CompilerParams(vmem_limit_bytes=56 * MIB),
        cost_estimate=pl.CostEstimate(
            flops=8 * 1024 * MIB, bytes_accessed=16 * MIB, transcendentals=4 * MIB
        ),
        name="attention_forward",
    )(windows, tok, seg, gain_attn, w_qkv, w_proj, gain_moe, w_router, slot_row)


def gelu_parts(x):
    density = jnp.exp(-0.5 * (x * x))
    t = 1.0 / (1.0 + (0.3275911 * 2.0**-0.5) * jnp.abs(x))
    poly = 0.5 * 1.061405429
    for factor in (-1.453152027, 1.421413741, -0.284496736, 0.254829592):
        poly = poly * t + 0.5 * factor
    tail = poly * t * density
    phi = jnp.where(x >= 0.0, 1.0 - tail, tail)
    return phi, x * density * 0.3989422804014327


def expert_kernel(
    capacity,
    received,
    gz,
    weights_in,
    weights_out,
    out,
    back,
    grads,
    rows,
    rows_t,
    gz_t,
    act,
    gpre,
    out_sum,
    back_sum,
    scaled,
):
    sources, padded, unused = rows.shape
    shards = weights_in.shape[0]

    @pl.loop(0, sources)
    def _(s):
        span = pl.ds(pl.multiple_of(s * padded, 16), padded)
        rows[s] = received[s]
        tail = received[s, padded - 16 :, :].astype(f32)
        gate = tail[13:14] + tail[14:15] + tail[15:16]
        gate = jnp.transpose(jnp.broadcast_to(gate, (LANES, D)))[:padded, :1]
        live = iota((padded, 1), 0) < capacity
        gate = jnp.where(live, gate, 0.0)
        scaled[span, :] = (gate * gz[s].astype(f32)).astype(bf16)
        live16 = iota((16, 1), 0) < 16 - (padded - capacity)
        rows[s, padded - 16 :, :] = jnp.where(live16, tail, 0.0).astype(bf16)
        out_sum[span, :] = jnp.zeros((padded, D), f32)
        back_sum[span, :] = jnp.zeros((padded, D), f32)

    for c in range(shards):

        @pl.loop(0, sources)
        def _(s):
            span = pl.ds(pl.multiple_of(s * padded, 16), padded)
            w_in = weights_in[c]
            w_out = weights_out[c]
            pre = dot(rows[s], w_in)
            phi, slope = gelu_parts(pre)
            act_low = (pre * phi).astype(bf16)
            act[span, :] = act_low
            out_sum[span, :] += dot(act_low, w_out)
            grad_pre = (dot_nt(scaled[span, :], w_out) * (phi + slope)).astype(bf16)
            gpre[span, :] = grad_pre
            back_sum[span, :] += dot_nt(grad_pre, w_in)
            if c == shards - 1:
                out[s] = out_sum[span, :].astype(bf16)
                back[s] = back_sum[span, :].astype(bf16)

        if c == 0:
            for s in range(sources):
                rows_t[:, s * padded : (s + 1) * padded] = jnp.transpose(rows[s])
                gz_t[:, s * padded : (s + 1) * padded] = jnp.transpose(
                    scaled[s * padded : (s + 1) * padded, :]
                )
        grads[c, :D, :] = dot(rows_t[...], gpre[...]).astype(bf16)
        grads[c, D:, :] = dot(gz_t[...], act[...]).astype(bf16)


def experts_apply(rows, gz, weights_in, weights_out, capacity):
    sources, padded, unused = rows.shape
    shards = weights_in.shape[0]
    hidden = weights_in.shape[2]
    total = sources * padded
    return pl.pallas_call(
        functools.partial(expert_kernel, capacity),
        out_shape=(
            jax.ShapeDtypeStruct(rows.shape, bf16),
            jax.ShapeDtypeStruct(rows.shape, bf16),
            jax.ShapeDtypeStruct((shards, 2 * D, hidden), bf16),
        ),
        scratch_shapes=[
            pltpu.VMEM(rows.shape, bf16),
            pltpu.VMEM((D, total), bf16),
            pltpu.VMEM((D, total), bf16),
            pltpu.VMEM((total, hidden), bf16),
            pltpu.VMEM((total, hidden), bf16),
            pltpu.VMEM((total, D), f32),
            pltpu.VMEM((total, D), f32),
            pltpu.VMEM((total, D), bf16),
        ],
        compiler_params=pltpu.CompilerParams(vmem_limit_bytes=60 * MIB),
        cost_estimate=pl.CostEstimate(
            flops=12 * total * D * hidden * shards, bytes_accessed=20 * MIB, transcendentals=0
        ),
        name="experts",
    )(rows, gz, weights_in, weights_out)


def backward_kernel(
    experts,
    windows,
    tok,
    seg,
    gain_attn,
    w_qkv,
    w_proj,
    gain_moe,
    w_router,
    slot_col,
    cot,
    normed_attn,
    packed,
    context,
    lse,
    residual,
    normed_moe,
    gates,
    returned,
    back,
    mixed,
    grad_tokens,
    grad_gains,
    grad_qkv,
    grad_proj,
    grad_router,
    seg_col,
    seg_row,
    router,
    grad_residual,
    grad_attn,
    grad_context,
    grad_logits,
    grad_k,
    grad_v,
    grad_packed,
):
    tokens = tok.shape[0]
    padded = returned.shape[1]
    seg_row[...] = seg[...].astype(f32)
    seg_col[...] = jnp.transpose(jnp.broadcast_to(seg_row[...], (LANES, tokens)))
    router[...] = jnp.zeros_like(router)
    router[:, :experts] = w_router[...]
    grad_gains[...] = jnp.zeros_like(grad_gains)

    @pl.loop(0, tokens // TILE)
    def _(i):
        rows = pl.ds(pl.multiple_of(i * TILE, TILE), TILE)
        grad_z = cot[rows, :].astype(f32)
        probs = gates[rows, :]
        slots = slot_col[rows, :]
        lane = iota((TILE, LANES), 1)
        rest = residual[rows, :]
        total = rest
        back_total = jnp.zeros((TILE, D), f32)
        grad_gates = jnp.zeros((TILE, LANES), f32)
        for e in range(experts):
            slot = slots[:, e : e + 1]
            chosen = (iota((TILE, padded), 1).astype(f32) == slot).astype(f32).astype(bf16)
            result = dot(chosen, returned[e])
            total = total + probs[:, e : e + 1] * result
            inner = jnp.sum(result * grad_z, axis=1, keepdims=True)
            grad_gates = grad_gates + jnp.where(lane == e, inner, 0.0)
            back_total = back_total + dot(chosen, back[e])
        mixed[rows, :] = total.astype(bf16)
        gate_inner = jnp.sum(probs * grad_gates, axis=1, keepdims=True)
        high, low = split2(probs * (grad_gates - gate_inner))
        grad_logits[rows, :LANES] = high
        grad_logits[rows, LANES:] = low
        grad_normed = back_total + dot_nt(high, router[...]) + dot_nt(low, router[...])
        normal, inverse = norm_parts(rest)
        grad_norm, grad_gain = norm_back(grad_normed, gain_moe[...], normal, inverse)
        grad_gains[1:2, :] += grad_gain
        grad_rest = grad_z + grad_norm
        grad_residual[rows, :] = grad_rest
        attn = grad_rest.astype(bf16)
        grad_attn[rows, :] = attn
        grad_context[rows, :] = dot_nt(attn, w_proj[...]).astype(bf16)

    both = dot_tn(normed_moe[...], grad_logits[...])
    grad_router[...] = both[:, :LANES] + both[:, LANES:]
    grad_proj[...] = dot_tn(context[...], grad_attn[...])
    grad_k[...] = jnp.zeros_like(grad_k)
    grad_v[...] = jnp.zeros_like(grad_v)

    @pl.loop(0, tokens // QB)
    def _(block):
        query = pl.multiple_of(block * QB, QB)

        def body(low, width):
            bias = window_bias(seg_col, seg_row, low, width, query)
            for pair in range(PAIRS):
                cols = pair * PAIR
                q = (stack_heads(packed[pl.ds(query, QB), cols : cols + PAIR]) * HEAD ** (-0.5)).astype(bf16)
                k = packed[pl.ds(low, width), D + cols : D + cols + PAIR]
                v = packed[pl.ds(low, width), 2 * D + cols : 2 * D + cols + PAIR]
                grad_c = stack_heads(grad_context[pl.ds(query, QB), cols : cols + PAIR])
                probs = jnp.exp(dot_nt(k, q) + bias - lse[pl.ds(block, 1), pair, :])
                grad_probs = dot_nt(v, grad_c)
                grad_v[pl.ds(low, width), cols : cols + PAIR] += dot(probs.astype(bf16), grad_c)
                weighted = probs * grad_probs
                inner = jnp.sum(weighted, axis=0, keepdims=True)
                grad_scores = (weighted - probs * inner).astype(bf16)
                grad_k[pl.ds(low, width), cols : cols + PAIR] += dot(grad_scores, q)
                grad_q = unstack_cols(dot_tn(k, grad_scores)) * HEAD ** (-0.5)
                grad_packed[pl.ds(query, QB), cols : cols + PAIR] = grad_q.astype(bf16)

        by_window(windows, block, body)

    @pl.loop(0, tokens // TILE)
    def _(i):
        rows = pl.ds(pl.multiple_of(i * TILE, TILE), TILE)
        grad_packed[rows, D : 2 * D] = grad_k[rows, :].astype(bf16)
        grad_packed[rows, 2 * D :] = grad_v[rows, :].astype(bf16)
        grad_normed = dot_nt(grad_packed[rows, :], w_qkv[...])
        normal, inverse = norm_parts(tok[rows, :].astype(f32))
        grad_norm, grad_gain = norm_back(grad_normed, gain_attn[...], normal, inverse)
        grad_gains[0:1, :] += grad_gain
        grad_tokens[rows, :] = grad_residual[rows, :] + grad_norm

    grad_qkv[...] = dot_tn(normed_attn[...], grad_packed[...])


def backward(experts, windows, *operands):
    tok = operands[0]
    tokens = tok.shape[0]
    vmem = pl.BlockSpec(memory_space=pltpu.VMEM)
    return pl.pallas_call(
        functools.partial(backward_kernel, experts),
        in_specs=[pl.BlockSpec(memory_space=pltpu.SMEM)] + [vmem] * len(operands),
        out_shape=(
            jax.ShapeDtypeStruct((tokens, D), bf16),
            jax.ShapeDtypeStruct((tokens, D), f32),
            jax.ShapeDtypeStruct((8, D), f32),
            jax.ShapeDtypeStruct((D, 3 * D), f32),
            jax.ShapeDtypeStruct((D, D), f32),
            jax.ShapeDtypeStruct((D, LANES), f32),
        ),
        scratch_shapes=[
            pltpu.VMEM((tokens, LANES), f32),
            pltpu.VMEM((1, tokens), f32),
            pltpu.VMEM((D, LANES), bf16),
            pltpu.VMEM((tokens, D), f32),
            pltpu.VMEM((tokens, D), bf16),
            pltpu.VMEM((tokens, D), bf16),
            pltpu.VMEM((tokens, 2 * LANES), bf16),
            pltpu.VMEM((tokens, D), f32),
            pltpu.VMEM((tokens, D), f32),
            pltpu.VMEM((tokens, 3 * D), bf16),
        ],
        compiler_params=pltpu.CompilerParams(vmem_limit_bytes=60 * MIB),
        cost_estimate=pl.CostEstimate(
            flops=30 * 1024 * MIB, bytes_accessed=30 * MIB, transcendentals=4 * MIB
        ),
        name="attention_backward",
    )(windows, *operands)


def per_device(
    tokens,
    segment_ids,
    expert_picks,
    priority_ranks,
    gain_attn,
    w_qkv,
    w_proj,
    gain_moe,
    w_router,
    w_in,
    w_out,
    cotangent,
):
    experts = w_router.shape[1]
    capacity = (21 * TOP * TOK_DEV + 20 * experts - 1) // (20 * experts)
    padded = (capacity + 3 + 15) // 16 * 16
    gain_attn = gain_attn.reshape(1, D)
    gain_moe = gain_moe.reshape(1, D)
    seg = segment_ids.reshape(1, SEQ)
    first = jnp.sum((segment_ids[None, :] < segment_ids[0::QB, None]).astype(jnp.int32), axis=1)
    after = jnp.sum((segment_ids[None, :] <= segment_ids[QB - 1 :: QB, None]).astype(jnp.int32), axis=1)
    low = jnp.minimum(first // 16 * 16, SEQ - WINDOW)
    fits = (after - low <= WINDOW).astype(jnp.int32)
    windows = jnp.concatenate([low, fits])

    slot_col, slot_row, counts, gz_send = route(
        expert_picks, priority_ranks, cotangent, experts, capacity, padded
    )
    gz = lax.all_to_all(gz_send, "wide", split_axis=0, concat_axis=0, tiled=True)
    gathered_in = lax.all_gather(w_in[0], "narrow", axis=0, tiled=False)
    gathered_out = lax.all_gather(w_out[0], "narrow", axis=0, tiled=False)
    normed_attn, packed, context, lse, residual, normed_moe, gates, rows_send = forward(
        windows, tokens, seg, gain_attn, w_qkv, w_proj, gain_moe, w_router, slot_row, padded
    )
    rows = lax.all_to_all(rows_send, "wide", split_axis=0, concat_axis=0, tiled=True)
    out, back, grads = experts_apply(rows, gz, gathered_in, gathered_out, capacity)
    returned = lax.all_to_all(out, "wide", split_axis=0, concat_axis=0, tiled=True)
    back = lax.all_to_all(back, "wide", split_axis=0, concat_axis=0, tiled=True)
    own = lax.psum_scatter(grads, "narrow", scatter_dimension=0, tiled=False).astype(f32)
    mixed, grad_tokens, grad_gains, grad_qkv, grad_proj, grad_router = backward(
        experts,
        windows,
        tokens,
        seg,
        gain_attn,
        w_qkv,
        w_proj,
        gain_moe,
        w_router,
        slot_col,
        cotangent,
        normed_attn,
        packed,
        context,
        lse,
        residual,
        normed_moe,
        gates,
        returned,
        back,
    )
    axes = ("wide", "narrow")
    grad_qkv, grad_proj = lax.psum((grad_qkv.astype(bf16), grad_proj.astype(bf16)), axes)
    grad_gains, grad_router, counts = lax.psum((grad_gains, grad_router[:, :experts], counts), axes)
    kept_counts = counts[0, :experts].astype(jnp.int32)
    dropped_counts = (counts[1, :experts] - counts[0, :experts]).astype(jnp.int32)
    return (
        mixed,
        grad_tokens,
        grad_gains[0],
        grad_qkv.astype(f32),
        grad_proj.astype(f32),
        grad_gains[1],
        grad_router,
        own[None, :D, :],
        own[None, D:, :].transpose(0, 2, 1),
        kept_counts,
        dropped_counts,
    )


def solution(mesh):
    both = ("wide", "narrow")
    placed = (
        P(both, None),
        P(both),
        P(both, None),
        P(both, None),
        P(),
        P(),
        P(),
        P(),
        P(),
        P("wide", None, "narrow"),
        P("wide", "narrow", None),
        P(both, None),
    )
    return jax.shard_map(
        per_device,
        mesh=mesh,
        in_specs=placed,
        out_specs=(
            P(both, None),
            P(both, None),
            P(),
            P(),
            P(),
            P(),
            P(),
            P("wide", None, "narrow"),
            P("wide", "narrow", None),
            P(),
            P(),
        ),
        check_vma=False,
    )
```

time: 725 us -> 494 us (0.68); the launches traced: 714 us -> 493 us
  matrix products: 277 us -> 0 us
  local copies, waits for them, and re-layouts: 157 us -> 9.37 us
  Pallas kernels: 0 us -> 139 us
  blocking collectives: 42 us -> 140 us
  other arithmetic: 93.9 us -> 12.5 us
  waiting for transfers between devices: 111 us -> 174 us
  starting transfers between devices: 18.8 us -> 5.45 us
    dot_general x22 -> x0, matrix products: 277 us -> none  [the longest x1 46.5 us: expert_back(): jnp.einsum('secd,efd->secf', grad_rows_in, weight_out, preferred_element_...]
    pallas_call x0 -> x4, Pallas kernels: none -> 139 us  [the longest x1 57 us: experts_apply(): pl.pallas_call(functools.partial(expert_kernel, capacity), out_shape=(jax...]
    all_to_all x0 -> x3, blocking collectives: none -> 96.5 us  [the longest x1 32.6 us: per_device(): lax.all_to_all(rows_send, 'wide', split_axis=0, concat_axis=0, tiled=True)]
    reduce_scatter x2 -> x1, waiting for transfers between devices: 0.01 us -> 73.6 us  [per_device(): lax.psum_scatter(grads, 'narrow', scatter_dimension=0, tiled=False)]
    gather x6 -> x0, local copies, waits for them, and re-layouts: 37.8 us -> none  [the longest x2 22.6 us: fetch_rows(): return padded[target]]
    reduce_sum x11 -> x1, other arithmetic: 34 us -> 0.23 us  [per_device(): jnp.sum((segment_ids[None, :] < segment_ids[0::QB, None]).astype(jnp.int3...]
    all_to_all x4 -> x1, waiting for transfers between devices: 25 us -> 0.01 us  [per_device(): lax.all_to_all(gz_send, 'wide', split_axis=0, concat_axis=0, tiled=True)]
    convert_element_type x7, other arithmetic: 33.8 us -> 11.7 us  [the longest x1 3.21 us: per_device(): grad_qkv.astype(bf16)]
  transfers between devices with their start and end apart: 9 -> 5, of which waited for: 2 -> 3; matrix products, arithmetic and copies ran while one was open for 55% -> 2% of each run, Pallas kernels for 0% -> 8%
where the time goes in v1:
time: 494 us; the launch traced here: 493 us
  waiting for transfers between devices  174 us (35%)
  blocking collectives  140 us (28%)
  Pallas kernels  139 us (28%)
  between operations  13.9 us (3%)
  other arithmetic  12.5 us (3%)
  local copies, waits for them, and re-layouts  9.37 us (2%)
  starting transfers between devices  5.45 us (1%)
    psum x1, waiting for transfers between devices, per_device(): lax.psum((grad_qkv.astype(bf16), grad_proj.astype(bf16)), axes)  85.5 us
    reduce_scatter x1, waiting for transfers between devices, per_device(): lax.psum_scatter(grads, 'narrow', scatter_dimension=0, tiled=False)  73.6 us
    pallas_call x1, Pallas kernels, experts_apply(): pl.pallas_call(functools.partial(expert_kernel, capacity), out_shape=(jax...  57 us
    psum x1, blocking collectives, per_device(): lax.psum((grad_gains, grad_router[:, :experts], counts), axes)  43.2 us
    pallas_call x1, Pallas kernels, backward(): pl.pallas_call(functools.partial(backward_kernel, experts), in_specs=[pl....  42.7 us
    pallas_call x1, Pallas kernels, forward(): pl.pallas_call(functools.partial(forward_kernel, experts), in_specs=[pl.B...  32.9 us
    all_to_all x1, blocking collectives, per_device(): lax.all_to_all(rows_send, 'wide', split_axis=0, concat_axis=0, tiled=True)  32.6 us
    all_to_all x1, blocking collectives, per_device(): lax.all_to_all(out, 'wide', split_axis=0, concat_axis=0, tiled=True)  32.5 us
  transfers between devices with their start and end apart: 5, of which 3 were waited for; matrix products, arithmetic and copies ran while one was open for 2% of the time, Pallas kernels for 8%

profile of v1, /device:TPU:0, one launch (start us, length us, event | category | flops | bytes accessed | tf_op | source)
XLA Modules:
  0.0 493.4 jit_solution(7139592370769229325)
XLA Ops:
  7.2 0.7 all-gather.3.cloned.1.call-update
  7.9 0.9 copy.33.picks
  8.8 1.2 copy-done
  10.1 0.7 copy-done.1
  10.7 6.3 %route.1 = (f32[1024,128]{1,0:T(8,128)S(1)}, f32[8,1024]{1,0:T(8,128)S(1)}, f32[8,128]{1,0:T(8,128)S(1)}, bf16[8,272,512]{2,1,0:T(8,128)(2,1)}) custom-call(s32[1024,2]{1,0:T(8,128)S(1)} %copy.33.picks, s32[1,1024]{1,0:T(1,128)S(1)} %copy-done.1, bf16[1024,512]{1,0:T(8,128)(2,1)S(1)} %copy-done), custom_call_target="tpu_custom_call" | custom-call | flops 2281701376 | bytes 6291456 | tf_op jit(solution)/shard_map/route/pallas_call | solution.py:108
  17.1 0.8 copy-done.2
  17.9 0.6 copy-done.3
  18.5 5.3 %all-to-all-start.1 = ((bf16[8,272,512]{2,1,0:T(8,128)(2,1)}), bf16[8,272,512]{2,1,0:T(8,128)(2,1)S(1)}, u32[]{:S(2)}, u32[]{:S(2)}) async-start(bf16[8,272,512]{2,1,0:T(8,128)(2,1)} %get-tuple-element.42), calls=%async_computation.1 | async-start | bytes 4456448 | tf_op jit(solution)/shard_map/all_to_all | solution.py:580
  23.9 0.7 all-gather.5.cloned.1.call-update
  25.0 0.8 copy.35.w_router
  25.8 0.6 pad_add_fusion.windows
  26.4 32.9 %attention_forward.1 = (bf16[1024,512]{1,0:T(8,128)(2,1)}, bf16[1024,1536]{1,0:T(8,128)(2,1)}, bf16[1024,512]{1,0:T(8,128)(2,1)}, f32[8,4,256]{2,1,0:T(4,128)}, ...) custom-call(s32[16]{0:T(128)} %pad_add_fusion.windows, ...), custom_call_target="tpu_custom_call" | custom-call | flops 8589934592 | bytes 16777216 | tf_op jit(solution)/shard_map/attention_forward/pallas_call | solution.py:258
  59.4 32.6 %all_to_all.20.received = bf16[8,272,512]{2,1,0:T(8,128)(2,1)} all-to-all(bf16[8,272,512]{2,1,0:T(8,128)(2,1)} %get-tuple-element.41), channel_id=1, replica_groups=mesh['wide'=8,'narrow'=4] {'wide'}, dimensions={0} | all-to-all | bytes 4456448 | tf_op jit(solution)/shard_map/all_to_all | solution.py:586
  92.0 12.5 %all-gather.5.cloned.1.call-done.weights_out = bf16[4,512,512]{2,1,0:T(8,128)(2,1)} async-done(((bf16[1,512,512]{2,1,0:T(8,128)(2,1)}), bf16[4,512,512]{2,1,0:T(8,128)(2,1)}) %all-gather.5.cloned.1.call-update) | async-done | bytes 2097168 | tf_op jit(solution)/shard_map/all_gather | solution.py:582
  104.5 57.0 %experts.1 = (bf16[8,272,512]{2,1,0:T(8,128)(2,1)}, bf16[8,272,512]{2,1,0:T(8,128)(2,1)}, bf16[4,1024,512]{2,1,0:T(8,128)(2,1)}) custom-call(bf16[8,272,512]{2,1,0:T(8,128)(2,1)} %all_to_all.20.received, bf16[8,272,512]{2,1,0:T(8,128)(2,1)} %copy-done.5, bf16[4,512,512]{2,1,0:T(8,128)(2,1)} %all-gather.3.cloned.1.call-done.weights_in, ...), custom_call_target="tpu_custom_call" | custom-call | flops 27380416512 | bytes 20971520 | tf_op jit(solution)/shard_map/experts/pallas_call | solution.py:367
  161.5 32.5 %all_to_all.21.returned = bf16[8,272,512]{2,1,0:T(8,128)(2,1)} all-to-all(bf16[8,272,512]{2,1,0:T(8,128)(2,1)} %get-tuple-element.43), channel_id=1, replica_groups=mesh['wide'=8,'narrow'=4] {'wide'}, dimensions={0} | all-to-all | bytes 4456448 | tf_op jit(solution)/shard_map/all_to_all | solution.py:588
  194.0 31.4 %all_to_all.22.back = bf16[8,272,512]{2,1,0:T(8,128)(2,1)} all-to-all(bf16[8,272,512]{2,1,0:T(8,128)(2,1)S(1)} %copy-done.6), channel_id=1, replica_groups=mesh['wide'=8,'narrow'=4] {'wide'}, dimensions={0} | all-to-all | bytes 4456448 | tf_op jit(solution)/shard_map/all_to_all | solution.py:589
  225.4 42.7 %attention_backward.1 = (bf16[1024,512]{1,0:T(8,128)(2,1)}, f32[1024,512]{1,0:T(8,128)}, f32[8,512]{1,0:T(8,128)}, f32[512,1536]{1,0:T(8,128)}, f32[512,512]{1,0:T(8,128)}, /*index=5*/f32[512,128]{1,0:T(8,128)}) custom-call(s32[16]{0:T(128)} %pad_add_fusion.windows, bf16[1024,512]{1,0:T(8,128)(2,1)} %tok.3, s32[1,1024]{1,0:T(1,128)} %bitcast.14, ...), custom_call_target="tpu_custom_call" | custom-call | flops 32212254720 | bytes 31457280 | tf_op jit(solution)/shard_map/attention_backward/pallas_call | solution.py:520
  268.1 2.1 convert_element_type.42
  270.2 3.2 convert_element_type.40
  273.5 0.5 reduce-scatter.2.cloned.1.call-update
  274.4 43.2 %all-reduce = (f32[8,512]{1,0:T(8,128)S(1)}, f32[512,8]{1,0:T(8,128)S(1)}, f32[8,128]{1,0:T(8,128)S(1)}) all-reduce(f32[8,512]{1,0:T(8,128)S(1)} %copy-done.9, f32[512,8]{1,0:T(8,128)S(1)} %bitcast.12, f32[8,128]{1,0:T(8,128)S(1)} %get-tuple-element.52), channel_id=1, replica_groups=mesh['wide'=8,'narrow'=4] {'wide','narrow'}, use_global_device_ids=true, to_apply=%region_2.3 | all-reduce | flops 9216 | bytes 73728 | tf_op jit(solution)/shard_map/psum | solution.py:615
  317.6 0.7 copy.36
  318.3 0.5 convert_bitcast_fusion
  318.8 0.6 fusion
  319.4 85.5 %all-reduce.4.cloned.1.call-done = (bf16[512,1536]{1,0:T(8,128)(2,1)}, bf16[512,512]{1,0:T(8,128)(2,1)}) async-done(((bf16[512,1536]{1,0:T(8,128)(2,1)}, bf16[512,512]{1,0:T(8,128)(2,1)}), (bf16[512,1536]{1,0:T(8,128)(2,1)}, bf16[512,512]{1,0:T(8,128)(2,1)})) %all-reduce.4.cloned.1.call-update) | async-done | bytes 2097168 | tf_op jit(solution)/shard_map/psum | solution.py:614
  404.9 2.3 convert_element_type.43
  407.2 2.1 convert_element_type.41
  409.3 73.6 %reduce-scatter.2.cloned.1.call-done = bf16[1,1024,512]{2,1,0:T(8,128)(2,1)} async-done(((bf16[4,1024,512]{2,1,0:T(8,128)(2,1)}), bf16[1,1024,512]{2,1,0:T(8,128)(2,1)}) %reduce-scatter.2.cloned.1.call-update) | async-done | bytes 1048592 | tf_op jit(solution)/shard_map/reduce_scatter | solution.py:590
  482.9 1.5 convert_element_type.44
  484.5 1.3 copy.37
  485.8 1.1 slice.41
  (32 shorter events, 1.1 us)
Async XLA Ops:
  7.2 84.8 %all-gather.3.cloned.1.call-start = ((), (), s32[]{:S(2)}) async-start(), calls=%async_computation.5 | async-start | bytes 2621440 | tf_op jit(solution)/shard_map/all_gather | solution.py:581
  8.8 1.2 copy-start
  10.1 0.7 copy-start.1
  17.1 0.8 copy-start.2
  17.9 0.6 copy-start.3
  18.5 6.1 %copy-start.11 = (s32[1024]{0:T(1024)S(1)}, s32[1024]{0:T(1024)}, u32[]{:S(2)}) copy-start(s32[1024]{0:T(1024)} %param.13) | copy-start | bytes 12292
  18.5 6.5 %copy-start.10 = (bf16[512,8]{0,1:T(8,128)(2,1)S(1)}, bf16[512,8]{0,1:T(8,128)(2,1)}, u32[]{:S(2)}) copy-start(bf16[512,8]{0,1:T(8,128)(2,1)} %param.20) | copy-start | bytes 24580
  18.5 40.8 %all-to-all-start.1 = ((bf16[8,272,512]{2,1,0:T(8,128)(2,1)}), bf16[8,272,512]{2,1,0:T(8,128)(2,1)S(1)}, u32[]{:S(2)}, u32[]{:S(2)}) async-start(bf16[8,272,512]{2,1,0:T(8,128)(2,1)} %get-tuple-element.42), calls=%async_computation.1 | async-start | bytes 4456448 | tf_op jit(solution)/shard_map/all_to_all | solution.py:580
  23.8 80.7 %all-gather.5.cloned.1.call-start = ((), (), s32[]{:S(2)}) async-start(), calls=%async_computation.6 | async-start | bytes 2621440 | tf_op jit(solution)/shard_map/all_gather | solution.py:582
  24.6 380.4 %all-reduce.4.cloned.1.call-start = ((), (), s32[]{:S(2)}) async-start(), calls=%async_computation.8 | async-start | bytes 4194304 | tf_op jit(solution)/shard_map/psum | solution.py:614
  59.4 32.6 %copy-start.5 = (bf16[8,272,512]{2,1,0:T(8,128)(2,1)}, bf16[8,272,512]{2,1,0:T(8,128)(2,1)S(1)}, u32[]{:S(2)}) copy-start(bf16[8,272,512]{2,1,0:T(8,128)(2,1)S(1)} %all-to-all-done.1.gz) | copy-start | bytes 6684676
  161.5 32.5 %copy-start.6 = (bf16[8,272,512]{2,1,0:T(8,128)(2,1)S(1)}, bf16[8,272,512]{2,1,0:T(8,128)(2,1)}, u32[]{:S(2)}) copy-start(bf16[8,272,512]{2,1,0:T(8,128)(2,1)} %get-tuple-element.44) | copy-start | bytes 6684676
  273.4 1.0 copy-start.8
  273.4 0.9 copy-start.9
  273.4 209.4 %reduce-scatter.2.cloned.1.call-start = ((), (), s32[]{:S(2)}) async-start(), calls=%async_computation.7 | async-start | bytes 5242880 | tf_op jit(solution)/shard_map/reduce_scatter | solution.py:590
  404.9 2.3 copy-start.7
  484.4 1.4 copy-start.4
Sparse Core Ops, SparseCore 0:
  9.6 48.6 all-gather.2
  59.8 44.6 all-gather.4
  273.5 131.3 all-reduce.3
  407.2 75.6 reduce-scatter.1
